TPU v7x, 32 devices: a whole 2x2x4 slice. The times are simulated.
32 devices in a mesh: img: 8 (over z, y), win: 4 (over x, core).
Axes of the slice: x: 2, y: 2, z: 4, core: 2. Of those that a mesh axis runs over, the one named last changes fastest.
Arguments:
- tokens: bfloat16 [256, 4, 49, 384], P('img', 'win'), may hold values from -6 to 6
- cotangent: bfloat16 [256, 4, 49, 384], P('img', 'win'), may hold values from -6 to 6
- crop_counts: int32 [8], P('img'), may hold values from 8 to 32, as said below
- crop_extent: int32 [256, 2], P('img'), may hold values from 10 to 14
- norm_gain: float32 [2, 2, 384], replicated, may hold values from 0.1 to 1.9
- norm_bias: float32 [2, 2, 384], replicated, may hold values from -3 to 3
- qkv_weight: bfloat16 [2, 384, 1152], replicated, may hold values from -0.3125 to 0.3125
- qv_bias: float32 [2, 2, 384], replicated, may hold values from -3 to 3
- rel_table: float32 [2, 169, 12], replicated, may hold values from -5 to 5
- proj_weight: bfloat16 [2, 384, 384], replicated, may hold values from -1.25 to 1.25
- out_bias: float32 [2, 2, 384], replicated, may hold values from -3 to 3
- fc1_weight: bfloat16 [2, 384, 1536], replicated, may hold values from -0.3125 to 0.3125
- fc1_bias: float32 [2, 1536], replicated, may hold values from -3 to 3
- fc2_weight: bfloat16 [2, 1536, 384], replicated, may hold values from -0.15625 to 0.15625
Outputs:
- output: bfloat16 [256, 4, 49, 384], P('img', 'win')
- input_grad: bfloat16 [256, 4, 49, 384], P('img', 'win')
- grad_norm_gain: float32 [2, 2, 384], replicated
- grad_norm_bias: float32 [2, 2, 384], replicated
- grad_qkv_weight: float32 [2, 384, 1152], replicated
- grad_qv_bias: float32 [2, 2, 384], replicated
- grad_rel_table: float32 [2, 169, 12], replicated
- grad_proj_weight: float32 [2, 384, 384], replicated
- grad_out_bias: float32 [2, 2, 384], replicated
- grad_fc1_weight: float32 [2, 384, 1536], replicated
- grad_fc1_bias: float32 [2, 1536], replicated
- grad_fc2_weight: float32 [2, 1536, 384], replicated
Inputs may be any that keep to these rules, and one draw needn't show every extreme that they name: `crop_counts`: slots of an image group from this count on are empty; in every draw some group is full.
All inputs are finite; a program needn't handle non-finite values.
Results may differ from a plain program's by a relative error of at most 0.017.
Values may be sent and summed in bfloat16 or wider, within the bound.
A program may use at most 256 MiB of HBM per device.

v0:
```python
import jax
import jax.numpy as jnp
from jax import lax
from jax.experimental import pallas as pl
from jax.experimental.pallas import tpu as pltpu
from jax.sharding import PartitionSpec as P

D = 384
FF = 1536
HEADS = 12
HEAD_DIM = 32
WINDOW = 7
SHIFT = 3
CELLS = WINDOW * WINDOW
SIDE = 2 * WINDOW
HALF = 16
ROWS = CELLS * HALF
LANES = 128
GROUPS = 3
KEYS = 56
SLOT = 64
SLABS = 12
SMALL = 16
TABLE = GROUPS * KEYS
SUMS = SLABS * D + 256
GROUPED = ((0, 1), (2, 3), (4, 5, 6))
NEG = -1e30
LOG2E = 1.4426950408889634
SCALE = HEAD_DIM**-0.5
MESH = pl.DeviceIdType.MESH

bf16 = jnp.bfloat16
f32 = jnp.float32
VMEM = pltpu.VMEM


def mm(a, b):
    return lax.dot_general(a, b, (((1,), (0,)), ((), ())), preferred_element_type=f32)


def mm_bt(a, b):
    return lax.dot_general(a, b, (((1,), (1,)), ((), ())), preferred_element_type=f32)


def mm_at(a, b):
    return lax.dot_general(a, b, (((0,), (0,)), ((), ())), preferred_element_type=f32)


def norm(x):
    centred = x - jnp.mean(x, -1, keepdims=True)
    rstd = lax.rsqrt(jnp.mean(centred * centred, -1, keepdims=True) + 1e-5)
    return centred * rstd, rstd


def norm_back(xh, rstd, dn, gain):
    e = dn * gain
    mean_e = jnp.mean(e, -1, keepdims=True)
    mean_ex = jnp.mean(e * xh, -1, keepdims=True)
    dx = rstd * (e - mean_e - xh * mean_ex)
    return dx, jnp.sum(dn * xh, 0, keepdims=True), jnp.sum(dn, 0, keepdims=True)


def gelu(u):
    phi = 0.5 + 0.5 * lax.erf(u * 0.7071067811865476)
    return u * phi, phi


def gelu_slope(u, phi):
    return phi + u * jnp.exp2(u * u * (-0.5 * LOG2E)) * 0.3989422804014327


def spread(rows):
    head = lax.broadcasted_iota(jnp.int32, rows.shape, 1) // HEAD_DIM
    zero = jnp.zeros_like(rows)
    return jnp.concatenate([jnp.where(head == h, rows, zero) for h in range(4)], 0)


def gather_heads(rows):
    head = lax.broadcasted_iota(jnp.int32, (KEYS, LANES), 1) // HEAD_DIM
    out = rows[:KEYS]
    for h in range(1, 4):
        out = jnp.where(head == h, rows[SLOT * h : SLOT * h + KEYS], out)
    return out


def to_windows(ref, slot, part):
    parted = part.reshape(CELLS, 2, 8, LANES)
    for cg in range(2):
        ref[cg, slot, 0 : CELLS * 8, :] = parted[:, cg].reshape(CELLS * 8, LANES)


def from_windows(ref, slot):
    parts = [ref[cg, slot, 0 : CELLS * 8, :].reshape(CELLS, 1, 8, LANES) for cg in range(2)]
    return jnp.concatenate(parts, 1).reshape(ROWS, LANES)


def cells(shifted):
    win = lax.axis_index("win")
    j = lax.broadcasted_iota(jnp.int32, (KEYS, LANES), 0)
    i = lax.broadcasted_iota(jnp.int32, (KEYS, LANES), 1) % SLOT
    top, left = WINDOW * (win // 2), WINDOW * (win % 2)
    places = [top + j // WINDOW, left + j % WINDOW, top + i // WINDOW, left + i % WINDOW]
    if not shifted:
        return places, None
    region = [(v >= SIDE - WINDOW).astype(jnp.int32) + (v >= SIDE - SHIFT).astype(jnp.int32) for v in places]
    apart = (region[0] != region[2]) | (region[1] != region[3])
    moved = [jnp.where(v + SHIFT >= SIDE, v + SHIFT - SIDE, v + SHIFT) for v in places]
    return moved, jnp.where(apart, NEG, 0.0)


def forward(step, block, shifted, x, refs, keep_n1=None, keep_n2=None, keep_gelu=None, keep_u=None):
    (ext, gain, beta, wqkv, qvb, bias, wp, ob, w1, b1, w2, xs, qw, pr, os, o16, mid) = refs
    xh, _ = norm(x)
    n1 = (xh * gain[block, 0:1, :] + beta[block, 0:1, :]).astype(bf16)
    if keep_n1 is not None:
        keep_n1[step] = n1
    proj = mm(n1, wqkv[...])
    q = (proj[:, :D] + qvb[block, 0:1, :]) * (SCALE * LOG2E)
    k = proj[:, D : 2 * D]
    v = proj[:, 2 * D :] + qvb[block, 1:2, :]
    for g in range(GROUPS):
        cut = slice(LANES * g, LANES * (g + 1))
        to_windows(xs, g, q[:, cut])
        to_windows(xs, GROUPS + g, k[:, cut])
        to_windows(xs, 2 * GROUPS + g, v[:, cut])
    places, apart = cells(shifted)
    if apart is not None:
        apart = jnp.concatenate([apart, apart], 1)

    def windows(part, carry):
        masks = []
        for w in [8 * part + n for n in range(8)]:
            rows, cols = ext[step * HALF + w, 0], ext[step * HALF + w, 1]
            valid_j = (places[0] < rows) & (places[1] < cols)
            valid_i = (places[2] < rows) & (places[3] < cols)
            mask = jnp.where(valid_i == valid_j, 0.0, NEG)
            mask = jnp.concatenate([mask, mask], 1)
            masks.append(mask if apart is None else mask + apart)
        for g in range(GROUPS):
            for n in range(8):
                w = 8 * part + n
                qs, ks, vs = (xs[part, GROUPS * m + g, pl.ds(n, SLOT, stride=8), :].astype(bf16) for m in range(3))
                for m, value in enumerate((qs, ks, vs)):
                    qw[w, GROUPS * m + g] = value
                s = mm_bt(ks[:KEYS], spread(qs)) + bias[g] + masks[n]
                e = jnp.exp2(s - jnp.max(s, 0, keepdims=True))
                p = (e * (1.0 / jnp.sum(e, 0, keepdims=True))).astype(bf16)
                pr[w, g] = p
                os[part, g, pl.ds(n, KEYS, stride=8), :] = gather_heads(mm_at(p, vs[:KEYS]))
        return carry

    lax.fori_loop(0, 2, windows, 0)
    for g in range(GROUPS):
        o16[:, LANES * g : LANES * (g + 1)] = from_windows(os, g).astype(bf16)
    middle = x + (mm(o16[...], wp[...]) + ob[block, 0:1, :])
    mid[...] = middle
    xh2, _ = norm(middle)
    n2 = (xh2 * gain[block, 1:2, :] + beta[block, 1:2, :]).astype(bf16)
    if keep_n2 is not None:
        keep_n2[step] = n2
    y = middle + ob[block, 1:2, :]
    for part in range(3):
        cut = slice(512 * part, 512 * (part + 1))
        u = mm(n2, w1[:, cut]) + b1[block : block + 1, cut]
        if keep_u is not None:
            keep_u[:, cut] = u.astype(bf16)
        z, phi = gelu(u)
        z = z.astype(bf16)
        if keep_gelu is not None:
            keep_gelu[0][step, :, cut] = z
            keep_gelu[1][:, cut] = gelu_slope(u, phi).astype(bf16)
        y = y + mm(z, w2[cut, :])
    return y


def no_tick(point, when=True):
    pass


def mlp_back(step, block, mid, dy, refs, slope, keep_n2=None, beta=None, tick=no_tick):
    (gain, wp, w1, w2, dos, dm_all, du_all, da_all, small) = refs

    def add_small(row, value):
        small[row : row + 1, :] += value

    dm = dy.astype(bf16)
    dm_all[step] = dm
    add_small(7, jnp.sum(dm.astype(f32), 0, keepdims=True))
    sums = []
    for part in range(3):
        cut = slice(512 * part, 512 * (part + 1))
        du = (mm_bt(dm, w2[cut, :]) * slope(cut)).astype(bf16)
        du_all[step, :, cut] = du
        sums.append(jnp.sum(du.astype(f32), 0, keepdims=True))
        tick(part)
    sums = jnp.concatenate(sums, 1)
    for part in range(4):
        add_small(8 + part, sums[:, D * part : D * (part + 1)])
    dn2 = mm_bt(du_all[step], w1[...])
    tick(3)
    xh, rstd = norm(mid)
    if keep_n2 is not None:
        keep_n2[step] = (xh * gain[block, 1:2, :] + beta[block, 1:2, :]).astype(bf16)
    dx, dgain, dbeta = norm_back(xh, rstd, dn2, gain[block, 1:2, :])
    add_small(1, dgain)
    add_small(3, dbeta)
    dmid = dy + dx
    da = dmid.astype(bf16)
    da_all[step] = da
    add_small(6, jnp.sum(da.astype(f32), 0, keepdims=True))
    do = mm_bt(da, wp[...])
    for g in range(GROUPS):
        to_windows(dos, g, do[:, LANES * g : LANES * (g + 1)])
    tick(4)
    return dmid


def attention_back(step, block, x, dmid, refs, keep_n1=None, beta=None, tick=no_tick):
    (gain, wqkv, xs, qw, pr, dos, dp_all, small, dbias) = refs

    def add_small(row, value):
        small[row : row + 1, :] += value

    def windows_back(part, carry):
        units = [(n, g) for n in range(8) for g in range(GROUPS)]
        grad, scores = {}, {}
        for n, g in units:
            grad[n, g] = spread(dos[part, g, pl.ds(n, SLOT, stride=8), :].astype(bf16))
        dprobs = {(n, g): mm_bt(qw[8 * part + n, 2 * GROUPS + g][:KEYS], grad[n, g]) for n, g in units}
        for g in range(GROUPS):
            total = jnp.zeros((KEYS, 4 * SLOT), f32)
            for n in range(8):
                p = pr[8 * part + n, g].astype(f32)
                t = p * dprobs[n, g]
                ds = t - p * jnp.sum(t, 0, keepdims=True)
                total = total + ds
                scores[n, g] = ds.astype(bf16)
            dbias[g] += total
        for n, g in units:
            w, ds = 8 * part + n, scores[n, g]
            dv = mm(pr[w, g], grad[n, g])
            dk = mm(ds, spread(qw[w, g])) * (1.0 / LOG2E)
            dq = gather_heads(mm_at(ds, qw[w, GROUPS + g][:KEYS])) * SCALE
            for m, value in enumerate((dq, dk, dv)):
                xs[part, GROUPS * m + g, pl.ds(n, KEYS, stride=8), :] = value
        for n in range(4):
            tick(n, part == n // 2)
        return carry

    lax.fori_loop(0, 2, windows_back, 0)
    for n in range(3 * GROUPS):
        dp_all[step, :, LANES * n : LANES * (n + 1)] = from_windows(xs, n).astype(bf16)
    dp = dp_all[step, :, : 3 * D]
    add_small(4, jnp.sum(dp[:, :D].astype(f32), 0, keepdims=True))
    add_small(5, jnp.sum(dp[:, 2 * D :].astype(f32), 0, keepdims=True))
    dn1 = mm_bt(dp, wqkv[...])
    tick(4)
    xh, rstd = norm(x)
    if keep_n1 is not None:
        keep_n1[step] = (xh * gain[block, 0:1, :] + beta[block, 0:1, :]).astype(bf16)
    dx, dgain, dbeta = norm_back(xh, rstd, dn1, gain[block, 0:1, :])
    add_small(0, dgain)
    add_small(2, dbeta)
    tick(5)
    return dmid() + dx


def flat(ref, cut=slice(None)):
    return ref[:, :, cut].reshape(2 * ROWS, -1)


def put_slabs(out, first, value):
    for j in range(value.shape[1] // D):
        out[D * (first + j) : D * (first + j + 1), :] = value[:, D * j : D * (j + 1)].astype(bf16)


def fc_grads(n2, z, dm, du, out, tick=no_tick):
    for first, left, right in ((0, n2, du), (4, dm, z)):
        for j in range(2):
            put_slabs(out, first + 2 * j, mm_at(flat(left), flat(right, slice(768 * j, 768 * (j + 1)))))
        tick(first // 4)


def attention_grads(n1, o16, da, dp, out):
    put_slabs(out, 8, mm_at(flat(n1), flat(dp, slice(3 * D))))
    put_slabs(out, 11, mm_at(flat(o16), flat(da)))


def small_grads(small, dbias, out):
    base = SLABS * D
    out[base : base + SMALL, :] = small[...].astype(bf16)
    out[base + SMALL : SUMS, :] = jnp.zeros((SUMS - base - SMALL, D), bf16)
    out[base + SMALL : base + SMALL + TABLE, : 4 * SLOT] = dbias[...].reshape(TABLE, 4 * SLOT).astype(bf16)


KEEP = WINDOW - SHIFT
NEAR, FAR = slice(0, KEEP), slice(KEEP, WINDOW)
HERE, THERE = slice(SHIFT, WINDOW), slice(0, SHIFT)


def shift_peers():
    win = lax.axis_index("win")
    beside = 1 - 2 * (win % 2)
    below = 2 - 4 * (win // 2 % 2)
    return [{"win": win + beside}, {"win": win + below}, {"win": win + beside + below}]


def shift_copies(source, target, send, recv, back=False):
    plain = [(HERE, HERE), (HERE, THERE), (THERE, HERE), (THERE, THERE)]
    moved = [(NEAR, NEAR), (NEAR, FAR), (FAR, NEAR), (FAR, FAR)]
    if back:
        plain, moved = moved, plain
    out = [pltpu.make_async_copy(source.at[plain[0]], target.at[moved[0]], send.at[3])]
    for n, to in enumerate(shift_peers()):
        out.append(
            pltpu.make_async_remote_copy(
                source.at[plain[n + 1]], target.at[moved[n + 1]], send.at[n], recv.at[n], device_id=to, device_id_type=MESH
            )
        )
    return out


def start_all(copies):
    for copy in copies:
        copy.start()


def wait_all(copies):
    for copy in copies:
        copy.wait()


def greet(peers):
    barrier = pltpu.get_barrier_semaphore()
    for to in peers:
        pl.semaphore_signal(barrier, inc=1, device_id=to, device_id_type=MESH)
    pl.semaphore_wait(barrier, len(peers))


def first_kernel(
    ext, x_ref, cot, gain, beta, wqkv, qvb, bias, wp, ob, w1, b1, w2,
    y_shifted, y_last, cot_shifted, qw, pr, o16, mid, u_ref, xs, os, y_first, send, recv,
):
    step = pl.program_id(0)
    cot_copies = shift_copies(cot, cot_shifted, send.at[0], recv.at[0])
    y_copies = shift_copies(y_first, y_shifted, send.at[1], recv.at[1])

    @pl.when(step == 0)
    def _():
        greet(shift_peers())
        start_all(cot_copies)
        xs[...] = jnp.zeros_like(xs)

    x = x_ref[...].reshape(ROWS, D).astype(f32)
    y = forward(
        step, 0, False, x, (ext, gain, beta, wqkv, qvb, bias, wp, ob, w1, b1, w2, xs, qw, pr, os, o16, mid), keep_u=u_ref
    )
    y = y.astype(bf16).reshape(WINDOW, WINDOW, HALF, D)

    @pl.when(step == 0)
    def _():
        y_first[...] = y
        start_all(y_copies)

    @pl.when(step == 1)
    def _():
        y_last[...] = y
        wait_all(y_copies)
        wait_all(cot_copies)


def second_kernel(
    ext, count, x_first, x_last, cot_ref, gain, beta, wqkv, qvb, bias, wp, ob, w1, b1, w2,
    y_ref, dx_shifted, dx_last, grads,
    xs, qw, pr, os, mid, slope, dos, small, dbias, n1, n2, o16, z, dm, du, da, dp, x_both, dx_first, send, recv, local,
):
    step = pl.program_id(0)
    x_copies = shift_copies(x_last, x_both.at[1], send.at[0], recv.at[0])
    dx_copies = shift_copies(dx_first, dx_shifted, send.at[1], recv.at[1], back=True)

    @pl.when(step == 0)
    def _():
        load = pltpu.make_async_copy(x_first, x_both.at[0], local)
        load.start()
        greet(shift_peers())
        start_all(x_copies)
        load.wait()
        xs[...] = jnp.zeros_like(xs)
        dos[...] = jnp.zeros_like(dos)
        small[...] = jnp.zeros_like(small)
        dbias[...] = jnp.zeros_like(dbias)

    @pl.when(step == 1)
    def _():
        wait_all(x_copies)

    x = x_both[step].reshape(ROWS, D).astype(f32)
    live = lax.broadcasted_iota(jnp.int32, (CELLS, HALF, 1), 1) + step * HALF < count[0]
    y = forward(
        step, 1, True, x,
        (ext, gain, beta, wqkv, qvb, bias, wp, ob, w1, b1, w2, xs, qw, pr, os, o16.at[step], mid),
        n1, n2, (z, slope),
    )
    y_ref[...] = jnp.where(live, y.reshape(CELLS, HALF, D), 0.0).astype(bf16)
    dy = jnp.where(live, cot_ref[...].astype(f32), 0.0).reshape(ROWS, D)
    mid[...] = mlp_back(
        step, 1, mid[...], dy, (gain, wp, w1, w2, dos, dm, du, da, small), lambda cut: slope[:, cut].astype(f32)
    )
    dx = attention_back(
        step, 1, x, lambda: mid[...], (gain, wqkv, xs, qw, pr, dos, dp, small, dbias)
    )
    dx = dx.astype(bf16).reshape(WINDOW, WINDOW, HALF, D)

    @pl.when(step == 0)
    def _():
        dx_first[...] = dx
        start_all(dx_copies)

    @pl.when(step == 1)
    def _():
        dx_last[...] = dx
        fc_grads(n2, z, dm, du, grads)
        attention_grads(n1, o16, da, dp, grads)
        small_grads(small, dbias, grads)
        wait_all(dx_copies)


LAST = 24
PACE = {
    (0, 0): (4.2, 6.0, 13.5, 17.1, 21.7, 32.9, 50.5),
    (0, 1): (1.9, 3.9, 9.1, 12.7, 16.3, 31.4, 37.3),
    (0, 2): (2.6, 4.5, 10.1, 13.9, 20.1, 40.0, 52.1),
    (1, 0): (30.7, 33.8, 38.5, 44.6, 47.5, 59.9, 73.1),
    (1, 1): (13.1, 17.1, 29.9, 42.0, 56.9, 72.9, 95.6),
    (1, 2): (29.3, 30.4, 38.3, 39.8, 46.6, 57.1, 68.4),
}


def schedule(*exchanges):
    out = []
    for (which, group), places in PACE.items():
        exchange = exchanges[which]
        if exchange.stages + 1 != len(places):
            first = LAST + 1 if which and group == 2 else places[0]
            places = [first + 4 * k + 0.1 * group for k in range(exchange.stages + 1)]
        out += [(place, exchange, group, k) for k, place in enumerate(places)]
    return sorted(out, key=lambda item: item[0])


def third_kernel(
    x_ref, dy_first, dy_last, y_ref, qw, pr, o_ref, mid, u_ref, gain, beta, wqkv, wp, w1, w2, two_ref,
    dx_ref, one_out, two_out, y_out,
    xs, dos, small, dbias, dmid, n2, o16, z, dm, du, da,
    one, two, land_one, send_one, recv_one, free_one, land_two, send_two, recv_two, free_two, local, loads, dy_both, send, recv,
):
    step = pl.program_id(0)
    first = Exchange(one, land_one, send_one, recv_one, free_one)
    second = Exchange(two, land_two, send_two, recv_two, free_two)
    dy_copies = shift_copies(dy_last, dy_both.at[1], send.at[0], recv.at[0], back=True)
    y_copies = shift_copies(y_ref, y_out, send.at[1], recv.at[1], back=True)
    moves = [[] for _ in range(LAST + 1)]
    late = []
    for place, exchange, group, k in schedule(second, first):
        (moves[int(place)] if place < LAST + 1 else late).append((exchange, group, k))

    def tick(n):
        if n == 14:
            start_all(y_copies)
        for exchange, group, k in moves[n]:
            exchange.advance(GROUPED[group], k)

    def tick_at(steps, base, per_step):
        def ticker(point, when=True):
            for s in steps:
                pl.when((step == s) & when)(lambda s=s: tick(base + (s - steps[0]) * per_step + point))

        return ticker

    def kept(half):
        rows = pl.ds(half * ROWS, ROWS)
        return (
            pltpu.make_async_copy(u_ref.at[rows], z.at[half], loads.at[0, half]),
            pltpu.make_async_copy(o_ref.at[rows], o16.at[half], loads.at[1, half]),
        )

    @pl.when(step == 0)
    def _():
        load = pltpu.make_async_copy(two_ref, two, local.at[0])
        load.start()
        load_dy = pltpu.make_async_copy(dy_first, dy_both.at[0], local.at[1])
        load_dy.start()
        for half in range(2):
            start_all(kept(half))
        greet(second.peers() + shift_peers()[2:])
        start_all(dy_copies)
        xs[...] = jnp.zeros_like(xs)
        dos[...] = jnp.zeros_like(dos)
        small[...] = jnp.zeros_like(small)
        dbias[...] = jnp.zeros_like(dbias)
        load.wait()
        tick(0)
        load_dy.wait()

    for half in range(2):

        @pl.when(step == half)
        def _():
            wait_all(kept(half))
            if half:
                wait_all(dy_copies)

    @pl.when(step < 2)
    def _():
        def slope(cut):
            u = z[step, :, cut].astype(f32)
            value, phi = gelu(u)
            z[step, :, cut] = value.astype(bf16)
            return gelu_slope(u, phi)

        dmid[step] = mlp_back(
            step, 0, mid[...], dy_both[step].astype(f32).reshape(ROWS, D),
            (gain, wp, w1, w2, dos.at[step], dm, du, da, small), slope, n2, beta, tick_at((0, 1), 1, 5),
        )

    @pl.when(step == 1)
    def _():
        fc_grads(n2, z, dm, du, one, lambda point: tick(11 + point))

    @pl.when(step >= 2)
    def _():
        half = step - 2
        dx = attention_back(
            half, 0, x_ref[...].reshape(ROWS, D).astype(f32), lambda: dmid[half],
            (gain, wqkv, xs, qw, pr, dos.at[half], du, small, dbias), n2, beta, tick_at((2, 3), 13, 6),
        )
        dx_ref[...] = dx.astype(bf16).reshape(dx_ref.shape)

    @pl.when(step == 3)
    def _():
        attention_grads(n2, o16, da, du, one)
        small_grads(small, dbias, one)
        for n, (exchange, group, k) in enumerate(late):
            exchange.advance(GROUPED[group], k)
            if all(other is not second for other, _, _ in late[n + 1 :]) and (exchange is second or n == 0):
                store_two = pltpu.make_async_copy(two, two_out, local.at[0])
                store_two.start()
        store_one = pltpu.make_async_copy(one, one_out, local.at[1])
        store_one.start()
        wait_all(y_copies)
        store_one.wait()
        store_two.wait()


def whole(shape):
    return pl.BlockSpec(shape, lambda s: (0,) * len(shape), pipeline_mode=pl.Buffered(1))


def of_block(block, *shape):
    return pl.BlockSpec((None,) + shape, lambda s: (block,) + (0,) * len(shape), pipeline_mode=pl.Buffered(1))


def by_half(*shape, buffers=2):
    return pl.BlockSpec(shape, lambda s: (s,) + (0,) * (len(shape) - 1), pipeline_mode=pl.Buffered(buffers))


ANY_SPEC = pl.BlockSpec(memory_space=pl.ANY)
SMEM_SPEC = pl.BlockSpec(memory_space=pltpu.SMEM)
TOKEN_SPEC = pl.BlockSpec((CELLS, HALF, D), lambda s: (0, s, 0))
XS = VMEM((2, 3 * GROUPS, 8 * SLOT, LANES), f32)
DOS = VMEM((2, GROUPS, 8 * SLOT, LANES), f32)
QW = (HALF, 3 * GROUPS, SLOT, LANES)
PR = (HALF, GROUPS, KEYS, 4 * SLOT)


def params(collective_id=None, mib=61):
    return pltpu.CompilerParams(
        vmem_limit_bytes=mib * 2**20, dimension_semantics=("arbitrary",), collective_id=collective_id,
        has_side_effects=collective_id is not None,
    )


CELL = (WINDOW, WINDOW)
PART = jax.ShapeDtypeStruct(CELL + (HALF, D), bf16)
SHIFTS = [pltpu.SemaphoreType.DMA((2, 4)), pltpu.SemaphoreType.DMA((2, 4))]


def run_first(ext, x, cot, gain, beta, wqkv, qvb, bias, wp, ob, w1, b1, w2):
    crops = x.shape[1]
    return pl.pallas_call(
        first_kernel,
        grid=(2,),
        out_shape=(
            PART,
            PART,
            jax.ShapeDtypeStruct(cot.shape, bf16),
            jax.ShapeDtypeStruct((crops,) + QW[1:], bf16),
            jax.ShapeDtypeStruct((crops,) + PR[1:], bf16),
            jax.ShapeDtypeStruct((2 * ROWS, D), bf16),
            jax.ShapeDtypeStruct((2 * ROWS, D), f32),
            jax.ShapeDtypeStruct((2 * ROWS, FF), bf16),
        ),
        in_specs=[
            SMEM_SPEC, TOKEN_SPEC, ANY_SPEC, whole(gain.shape), whole(beta.shape), of_block(0, D, 3 * D), whole(qvb.shape),
            of_block(0, GROUPS, KEYS, 4 * SLOT), of_block(0, D, D), whole(ob.shape), of_block(0, D, FF),
            whole(b1.shape), of_block(0, FF, D),
        ],
        out_specs=(
            ANY_SPEC, whole(PART.shape), ANY_SPEC, by_half(*QW), by_half(*PR), by_half(ROWS, D), by_half(ROWS, D),
            by_half(ROWS, FF),
        ),
        scratch_shapes=[
            XS, VMEM((2, GROUPS, 8 * KEYS, LANES), f32), VMEM(PART.shape, bf16),
        ] + SHIFTS,
        compiler_params=params(1),
        name="first_forward",
    )(ext, x, cot, gain, beta, wqkv, qvb, bias, wp, ob, w1, b1, w2)


GRADS = jax.ShapeDtypeStruct((SUMS, D), bf16)
SMALLS = [VMEM((SMALL, D), f32), VMEM((GROUPS, KEYS, 4 * SLOT), f32)]


def run_second(ext, count, x_first, x_last, cot, gain, beta, wqkv, qvb, bias, wp, ob, w1, b1, w2):
    return pl.pallas_call(
        second_kernel,
        grid=(2,),
        out_shape=(jax.ShapeDtypeStruct(cot.shape, bf16), PART, PART, GRADS),
        in_specs=[
            SMEM_SPEC, SMEM_SPEC, ANY_SPEC, ANY_SPEC, TOKEN_SPEC, whole(gain.shape), whole(beta.shape), of_block(1, D, 3 * D),
            whole(qvb.shape), of_block(1, GROUPS, KEYS, 4 * SLOT), of_block(1, D, D), whole(ob.shape),
            of_block(1, D, FF), whole(b1.shape), of_block(1, FF, D),
        ],
        out_specs=(TOKEN_SPEC, ANY_SPEC, whole(PART.shape), whole(GRADS.shape)),
        scratch_shapes=[
            XS, VMEM(QW, bf16), VMEM(PR, bf16), VMEM((2, GROUPS, 8 * KEYS, LANES), f32),
            VMEM((ROWS, D), f32), VMEM((ROWS, FF), bf16), DOS,
        ] + SMALLS + [VMEM((2, ROWS, width), bf16) for width in (D, D, D, FF, D, FF, D, 3 * D)]
        + [VMEM((2,) + PART.shape, bf16), VMEM(PART.shape, bf16)] + SHIFTS + [pltpu.SemaphoreType.DMA(())],
        compiler_params=params(2, 63),
        name="second_block",
    )(ext, count, x_first, x_last, cot, gain, beta, wqkv, qvb, bias, wp, ob, w1, b1, w2)


def in_steps(first, *shape, axis=0, buffers=2):
    def index(s):
        return tuple(jnp.clip(s - first, 0, 1) if n == axis else 0 for n in range(len(shape)))

    return pl.BlockSpec(shape, index, pipeline_mode=pl.Buffered(buffers))


def run_third(x, dy_first, dy_last, y, qw, pr, o16, mid, u, gain, beta, wqkv, wp, w1, w2, two):
    tokens = (CELLS, HALF, D)
    return pl.pallas_call(
        third_kernel,
        grid=(4,),
        out_shape=(jax.ShapeDtypeStruct(x.shape, bf16), GRADS, GRADS, jax.ShapeDtypeStruct(y.shape, bf16)),
        in_specs=[
            in_steps(2, *tokens, axis=1), ANY_SPEC, ANY_SPEC, ANY_SPEC, in_steps(2, *QW, buffers=1),
            in_steps(2, *PR, buffers=1), ANY_SPEC, in_steps(0, ROWS, D), ANY_SPEC,
            whole(gain.shape), whole(beta.shape), of_block(0, D, 3 * D), of_block(0, D, D), of_block(0, D, FF),
            of_block(0, FF, D), ANY_SPEC,
        ],
        out_specs=(in_steps(2, *tokens, axis=1), ANY_SPEC, ANY_SPEC, ANY_SPEC),
        scratch_shapes=[XS, VMEM((2,) + DOS.shape, f32)] + SMALLS + [VMEM((2, ROWS, D), f32)]
        + [VMEM((2, ROWS, width), bf16) for width in (D, D, FF, D, FF, D)]
        + [VMEM(GRADS.shape, bf16)] * 2 + exchange_scratch() * 2
        + [pltpu.SemaphoreType.DMA((2,)), pltpu.SemaphoreType.DMA((2, 2)), VMEM((2,) + PART.shape, bf16)] + SHIFTS,
        compiler_params=params(0, 63),
        name="first_backward",
    )(x, dy_first, dy_last, y, qw, pr, o16, mid, u, gain, beta, wqkv, wp, w1, w2, two)


def jobs():
    n_img, n_win = lax.axis_size("img"), lax.axis_size("win")
    bits = [("win", b) for b in range(1, n_win.bit_length() - 1)] + [("img", b) for b in range(n_img.bit_length() - 1)]
    pairs = [bits[n : n + 2] for n in range(0, len(bits), 2)]
    orders = [[[("win", 0)]] + pairs, [[("win", 0)]] + pairs[::-1]]
    out = []
    for group in range(3):
        out += [(1536 * group, 1024, orders[0]), (1536 * group + 1024, 512, orders[1])]
    return out + [(SLABS * D, SUMS - SLABS * D, orders[0])]


def plan_sizes(size, order):
    out = []
    for group in order:
        ways = 2 ** len(group)
        cut = ways if size % (16 * ways) == 0 else 1
        size //= cut
        out.append((ways, cut, size))
    return out


class Exchange:
    def __init__(self, buf, landing, send, recv, free):
        self.buf, self.landing, self.send, self.recv, self.free = buf, landing, send, recv, free
        index = {axis: lax.axis_index(axis) for axis in ("img", "win")}
        self.plans, land = [], 0
        for start, rows, order in jobs():
            plan = []
            for group, (ways, cut, size) in zip(order, plan_sizes(rows, order)):
                own = [(index[axis] // 2**bit) % 2 for axis, bit in group]
                peers = []
                for apart in range(1, ways):
                    to, piece = {}, 0
                    for n, (axis, bit) in enumerate(group):
                        here = own[n]
                        if apart >> n & 1:
                            to[axis] = to.get(axis, index[axis]) + 2**bit - 2 ** (bit + 1) * here
                            here = 1 - here
                        piece = piece + here * 2**n
                    peers.append((to, start + piece * size if cut > 1 else start, land))
                    land += size
                if cut > 1:
                    start = start + sum(here * 2**n for n, here in enumerate(own)) * size
                plan.append((start, size, cut, peers))
            self.plans.append(plan)
        self.bits = len(self.plans[0])
        self.stages = 2 * self.bits

    def peers(self):
        return [to for *_, peers in self.plans[0] for to, _, _ in peers]

    def copies(self, c, k):
        n = min(k, self.stages - 1 - k)
        keep, size, cut, peers = self.plans[c][n]
        if k >= self.bits and cut == 1:
            return []
        out = []
        for p, (to, give, land) in enumerate(peers):
            if k < self.bits:
                source, target = self.buf.at[pl.ds(pl.multiple_of(give, 16), size)], self.landing.at[pl.ds(land, size)]
            else:
                source = target = self.buf.at[pl.ds(pl.multiple_of(keep, 16), size)]
            out.append(
                pltpu.make_async_remote_copy(
                    source, target, self.send.at[c, k, p], self.recv.at[c, k, p], device_id=to, device_id_type=MESH
                )
            )
        return out

    def start(self, c, k):
        copies = self.copies(c, k)
        if copies and k >= self.bits:
            pl.semaphore_wait(self.free.at[c, self.stages - 1 - k], len(copies))
        for copy in copies:
            copy.start()

    def finish(self, c, k):
        for copy in self.copies(c, k):
            copy.wait()
        if k >= self.bits:
            return
        keep, size, cut, peers = self.plans[c][k]
        if cut > 1:
            for to, _, _ in peers:
                pl.semaphore_signal(self.free.at[c, k], inc=1, device_id=to, device_id_type=MESH)
        tile = max(t for t in (16, 32, 48, 64) if size % t == 0)

        def add(i, carry):
            here = pl.ds(pl.multiple_of(keep + i * tile, 16), tile)
            total = self.buf[here, :].astype(f32)
            for _, _, land in peers:
                total = total + self.landing[pl.ds(pl.multiple_of(land + i * tile, 16), tile), :].astype(f32)
            self.buf[here, :] = total.astype(bf16)
            return carry

        lax.fori_loop(0, size // tile, add, 0)

    def advance(self, which, k):
        for c in which:
            if 1 <= k <= self.stages:
                self.finish(c, k - 1)
            if k < self.stages:
                self.start(c, k)


def exchange_scratch():
    landing, most = 0, 0
    for _, rows, order in jobs():
        for ways, _, size in plan_sizes(rows, order):
            landing += size * (ways - 1)
            most = max(most, ways - 1)
    n, bits = len(jobs()), len(jobs()[0][2])
    dma = pltpu.SemaphoreType.DMA((n, 2 * bits, most))
    return [VMEM((landing, D), bf16), dma, dma, pltpu.SemaphoreType.REGULAR((n, bits))]


def finish_kernel(*refs):
    ins, outs = refs[:8], refs[8:]
    for n, out in enumerate(outs):
        for block in range(2):
            value = ins[2 * n + block][...].astype(f32)
            out[block] = value.T if n == 1 else value


def finish(grads_one, grads_two):
    slabs = [lambda j: (j, 0), lambda j: (4 + j, 0), lambda j: (8 + jnp.minimum(j, 2), 0), lambda j: (11, 0)]
    targets = [lambda j: (0, 0, j), lambda j: (0, j, 0), lambda j: (0, 0, jnp.minimum(j, 2)), lambda j: (0, 0, 0)]
    return pl.pallas_call(
        finish_kernel,
        grid=(4,),
        out_shape=tuple(jax.ShapeDtypeStruct((2,) + s, f32) for s in ((D, FF), (FF, D), (D, 3 * D), (D, D))),
        in_specs=[pl.BlockSpec((D, D), index) for index in slabs for _ in range(2)],
        out_specs=tuple(pl.BlockSpec((2, D, D), index) for index in targets),
        compiler_params=params(),
        name="finish_gradients",
    )(*[grads_one, grads_two] * 4)


def position_lookup():
    j = jnp.arange(KEYS)[:, None]
    i = jnp.arange(SLOT)[None, :]
    side = SIDE - 1
    index = (i // WINDOW - j // WINDOW + WINDOW - 1) * side + i % WINDOW - j % WINDOW + WINDOW - 1
    index = jnp.where((i < CELLS) & (j < CELLS), index, -1).reshape(-1)
    return (jnp.arange(side * side)[:, None] == index[None, :]).astype(f32)


def on_device(
    tokens, cotangent, crop_counts, crop_extent, norm_gain, norm_bias, qkv_weight, qv_bias, rel_table, proj_weight,
    out_bias, fc1_weight, fc1_bias, fc2_weight,
):
    crops = tokens.shape[0]
    x = tokens.reshape(crops, CELLS, D).transpose(1, 0, 2)
    cot = cotangent.reshape(crops, CELLS, D).transpose(1, 0, 2)
    lookup = position_lookup()
    highest = lax.Precision.HIGHEST
    bias = jnp.einsum("bkh,kp->bhp", rel_table, lookup, precision=highest) * LOG2E
    bias = bias.reshape(2, GROUPS, 4, KEYS, SLOT).transpose(0, 1, 3, 2, 4)
    bias = jnp.where(jnp.arange(KEYS)[:, None, None] < CELLS, bias, NEG).reshape(2, GROUPS, KEYS, 4 * SLOT)

    cells_of = lambda v: v.reshape(CELL + v.shape[1:])
    rows_of = lambda v: v.reshape((CELLS,) + v.shape[2:])
    x_first, x_last, cot_shifted, qw, pr, o16, mid, u = run_first(
        crop_extent, x, cells_of(cot), norm_gain, norm_bias, qkv_weight, qv_bias, bias, proj_weight, out_bias,
        fc1_weight, fc1_bias, fc2_weight,
    )
    y, dx_first, dx_last, grads_two = run_second(
        crop_extent, crop_counts, x_first, x_last, rows_of(cot_shifted), norm_gain, norm_bias, qkv_weight, qv_bias,
        bias, proj_weight, out_bias, fc1_weight, fc1_bias, fc2_weight,
    )
    dx, sum_one, sum_two, output = run_third(
        x, dx_first, dx_last, cells_of(y), qw, pr, o16, mid, u, norm_gain, norm_bias, qkv_weight, proj_weight,
        fc1_weight, fc2_weight, grads_two,
    )
    fc1, fc2, qkv, proj = finish(sum_one, sum_two)
    rows = jnp.stack([sum_one[SLABS * D :], sum_two[SLABS * D :]]).astype(f32)
    dbias = rows[:, SMALL : SMALL + TABLE, : 4 * SLOT].reshape(2, GROUPS, KEYS, 4, SLOT).transpose(0, 1, 3, 2, 4)
    table = jnp.einsum("hp,kp->kh", dbias.reshape(2 * HEADS, KEYS * SLOT), lookup, precision=highest)
    table = table.reshape(-1, 2, HEADS).transpose(1, 0, 2)
    back = lambda v: v.transpose(1, 0, 2).reshape(tokens.shape)
    return (
        back(rows_of(output)), back(dx), rows[:, 0:2], rows[:, 2:4], qkv, rows[:, 4:6], table, proj, rows[:, 6:8], fc1,
        rows[:, 8:12].reshape(2, FF), fc2,
    )


def solution(mesh):
    split = P("img", "win", None, None)
    return jax.shard_map(
        on_device,
        mesh=mesh,
        in_specs=(split, split, P("img"), P("img", None)) + (P(),) * 10,
        out_specs=(split, split) + (P(),) * 10,
        check_vma=False,
    )
```

profile of v0, /device:TPU:0, one launch (start us, length us, event | category | flops | bytes accessed | tf_op | source)
XLA Modules:
  0.0 225.5 jit_solution(11863176501670972349)
XLA Ops:
  1.4 1.4 copy.36.ext
  2.7 0.1 add_select_fusion
  2.8 0.1 reshape.215
  2.9 1.1 fusion
  4.0 0.3 copy.33
  4.3 0.4 reshape.202
  4.7 0.1 select_bitcast_fusion
  4.9 0.3 copy.34
  5.1 1.2 reshape.203.bias
  6.3 26.9 %first_forward.1 = (bf16[7,7,16,384]{3,2,1,0:T(8,128)(2,1)}, bf16[7,7,16,384]{3,2,1,0:T(8,128)(2,1)}, bf16[7,7,32,384]{3,2,1,0:T(8,128)(2,1)}, bf16[32,9,64,128]...) custom-call(s32[32,2]{1,0:T(8,128)} %copy.36.ext, ...), custom_call_target="tpu_custom_call" | custom-call | tf_op jit(solution)/shard_map/first_forward/pallas_call | solution.py:589
  33.2 61.8 %second_block.1 = (bf16[49,32,384]{2,1,0:T(8,128)(2,1)}, bf16[7,7,16,384]{3,2,1,0:T(8,128)(2,1)}, bf16[7,7,16,384]{3,2,1,0:T(8,128)(2,1)}, bf16[4864,384]{1,0:T(8,128)(2,1)}) custom-call(s32[32,2]{1,0:T(8,128)} %copy.36.ext, s32[1]{0:T(128)S(6)} %copy.49.count, bf16[7,7,16,384]{3,2,1,0:T(8,128)(2,1)} %get-tuple-element.32.x_first, ...), custom_call_target="tpu_custom_call" | custom-call | tf_op jit(solution)/shard_map/second_block/pallas_call | solution.py:624
  95.0 113.9 %first_backward.1 = (bf16[49,32,384]{2,1,0:T(8,128)(2,1)}, bf16[4864,384]{1,0:T(8,128)(2,1)}, bf16[4864,384]{1,0:T(8,128)(2,1)}, bf16[7,7,32,384]{3,2,1,0:T(8,128)(2,1)}) custom-call(bf16[49,32,384]{2,1,0:T(8,128)(2,1)} %bitcast.47, bf16[7,7,16,384]{3,2,1,0:T(8,128)(2,1)} %get-tuple-element.35.dy_first, bf16[7,7,16,384]{3,2,1,0:T(8,128)(2,1)} %get-tuple-element.36.dy_last, ...), custom_call_target="tpu_custom_call" | custom-call | tf_op jit(solution)/shard_map/first_backward/pallas_call | solution.py:653
  208.9 0.9 slice_bitcast_fusion.1
  209.9 0.9 slice_bitcast_fusion
  210.9 0.2 reshape.209
  211.1 0.2 dot_general.9
  211.4 0.6 fusion.7
  211.9 0.6 copy.39
  212.6 0.6 fusion.14
  213.2 0.6 copy.40
  213.8 8.7 %finish_gradients.1 = (f32[2,384,1536]{2,1,0:T(8,128)}, f32[2,1536,384]{2,1,0:T(8,128)}, f32[2,384,1152]{2,1,0:T(8,128)}, f32[2,384,384]{2,1,0:T(8,128)}) custom-call(bf16[4864,384]{1,0:T(8,128)(2,1)} %get-tuple-element.46.refs_0_.refs_2_.refs_4_.refs_6_, bf16[4864,384]{1,0:T(8,128)(2,1)} %get-tuple-element.47.refs_1_.refs_3_.refs_5_.refs_7_, ...), custom_call_target="tpu_custom_call" | custom-call | tf_op jit(solution)/shard_map/finish_gradients/pallas_call | solution.py:800
  222.6 1.0 copy.50
  223.6 0.7 copy-done.1
  224.3 1.0 copy.51
  (13 shorter events, 0.2 us)
Async XLA Ops:
  0.6 2.3 %copy-start = (f32[2,169,12]{1,0,2:T(2,128)S(1)}, f32[2,169,12]{1,0,2:T(2,128)}, u32[]{:S(2)}) copy-start(f32[2,169,12]{1,0,2:T(2,128)} %param.22) | copy-start | bytes 48676
  213.8 8.7 %copy-start.2 = (bf16[7,7,32,384]{3,2,1,0:T(8,128)(2,1)S(1)}, bf16[7,7,32,384]{3,2,1,0:T(8,128)(2,1)}, u32[]{:S(2)}) copy-start(bf16[7,7,32,384]{3,2,1,0:T(8,128)(2,1)} %get-tuple-element.44) | copy-start | bytes 3612676
  222.6 1.7 copy-start.1
where the time goes:
time: 227 us; the launch traced here: 226 us
  Pallas kernels  211 us (93%)
  local copies, waits for them, and re-layouts  10.5 us (5%)
    pallas_call x1, Pallas kernels, run_third(): pl.pallas_call(third_kernel, grid=(4,), out_shape=(jax.ShapeDtypeStruct(x...  114 us
    pallas_call x1, Pallas kernels, run_second(): pl.pallas_call(second_kernel, grid=(2,), out_shape=(jax.ShapeDtypeStruct(...  61.8 us
    pallas_call x1, Pallas kernels, run_first(): pl.pallas_call(first_kernel, grid=(2,), out_shape=(PART, PART, jax.ShapeD...  26.9 us
    pallas_call x1, Pallas kernels, finish(): pl.pallas_call(finish_kernel, grid=(4,), out_shape=tuple((jax.ShapeDtypeS...  8.73 us
    unnamed x12, local copies, waits for them, and re-layouts  5.35 us

commit v1 on v0

--- a/solution.py
+++ b/solution.py
@@ -130,7 +130,7 @@
     def windows(part, carry):
         masks = []
         for w in [8 * part + n for n in range(8)]:
-            rows, cols = ext[step * HALF + w, 0], ext[step * HALF + w, 1]
+            rows, cols = ext[0, step * HALF + w], ext[1, step * HALF + w]
             valid_j = (places[0] < rows) & (places[1] < cols)
             valid_i = (places[2] < rows) & (places[3] < cols)
             mask = jnp.where(valid_i == valid_j, 0.0, NEG)
@@ -449,7 +449,7 @@
 
 def third_kernel(
     x_ref, dy_first, dy_last, y_ref, qw, pr, o_ref, mid, u_ref, gain, beta, wqkv, wp, w1, w2, two_ref,
-    dx_ref, one_out, two_out, y_out,
+    dx_ref, one_out, two_out, y_out, small_out,
     xs, dos, small, dbias, dmid, n2, o16, z, dm, du, da,
     one, two, land_one, send_one, recv_one, free_one, land_two, send_two, recv_two, free_two, local, loads, dy_both, send, recv,
 ):
@@ -546,6 +546,12 @@
                 store_two.start()
         store_one = pltpu.make_async_copy(one, one_out, local.at[1])
         store_one.start()
+        tails = [
+            pltpu.make_async_copy(ref.at[pl.ds(SLABS * D, SUMS - SLABS * D)], small_out.at[n], loads.at[0, n])
+            for n, ref in enumerate((one, two))
+        ]
+        start_all(tails)
+        wait_all(tails)
         wait_all(y_copies)
         store_one.wait()
         store_two.wait()
@@ -653,14 +659,17 @@
     return pl.pallas_call(
         third_kernel,
         grid=(4,),
-        out_shape=(jax.ShapeDtypeStruct(x.shape, bf16), GRADS, GRADS, jax.ShapeDtypeStruct(y.shape, bf16)),
+        out_shape=(
+            jax.ShapeDtypeStruct(x.shape, bf16), GRADS, GRADS, jax.ShapeDtypeStruct(y.shape, bf16),
+            jax.ShapeDtypeStruct((2, SUMS - SLABS * D, D), bf16),
+        ),
         in_specs=[
             in_steps(2, *tokens, axis=1), ANY_SPEC, ANY_SPEC, ANY_SPEC, in_steps(2, *QW, buffers=1),
             in_steps(2, *PR, buffers=1), ANY_SPEC, in_steps(0, ROWS, D), ANY_SPEC,
             whole(gain.shape), whole(beta.shape), of_block(0, D, 3 * D), of_block(0, D, D), of_block(0, D, FF),
             of_block(0, FF, D), ANY_SPEC,
         ],
-        out_specs=(in_steps(2, *tokens, axis=1), ANY_SPEC, ANY_SPEC, ANY_SPEC),
+        out_specs=(in_steps(2, *tokens, axis=1),) + (ANY_SPEC,) * 4,
         scratch_shapes=[XS, VMEM((2,) + DOS.shape, f32)] + SMALLS + [VMEM((2, ROWS, D), f32)]
         + [VMEM((2, ROWS, width), bf16) for width in (D, D, FF, D, FF, D)]
         + [VMEM(GRADS.shape, bf16)] * 2 + exchange_scratch() * 2
@@ -787,25 +796,50 @@
 
 
 def finish_kernel(*refs):
-    ins, outs = refs[:8], refs[8:]
-    for n, out in enumerate(outs):
-        for block in range(2):
-            value = ins[2 * n + block][...].astype(f32)
-            out[block] = value.T if n == 1 else value
-
-
-def finish(grads_one, grads_two):
-    slabs = [lambda j: (j, 0), lambda j: (4 + j, 0), lambda j: (8 + jnp.minimum(j, 2), 0), lambda j: (11, 0)]
-    targets = [lambda j: (0, 0, j), lambda j: (0, j, 0), lambda j: (0, 0, jnp.minimum(j, 2)), lambda j: (0, 0, 0)]
+    ins, (small, *sources), outs, smalls, targets = refs[:8], refs[8:11], refs[11:15], refs[15:20], refs[20:22]
+    step = pl.program_id(0)
+
+    @pl.when(step == 0)
+    def _():
+        rows = small[:, :SMALL].astype(f32)
+        for n, out in enumerate(smalls[:4]):
+            out[...] = rows[:, 2 * n : 2 * n + 2]
+        for n in range(4):
+            smalls[4][:, D * n : D * (n + 1)] = rows[:, 8 + n]
+
+    for source, target in zip(sources, targets):
+        target[...] = source[...]
+
+    @pl.when(step < 4)
+    def _():
+        for n, out in enumerate(outs):
+            for block in range(2):
+                value = ins[2 * n + block][...].astype(f32)
+                out[block] = value.T if n == 1 else value
+
+
+def finish(grads_one, grads_two, small, *passed):
+    first = [lambda j: jnp.minimum(j, 3), lambda j: 4 + jnp.minimum(j, 3), lambda j: 8 + jnp.minimum(j, 2), lambda j: 11]
+    places = [
+        lambda j: (0, 0, jnp.minimum(j, 3)), lambda j: (0, jnp.minimum(j, 3), 0), lambda j: (0, 0, jnp.minimum(j, 2)),
+        lambda j: (0, 0, 0),
+    ]
+    small_shapes = [(2, 2, D)] * 4 + [(2, FF)]
+    tokens = pl.BlockSpec((WINDOW,) + passed[0].shape[1:], lambda j: (j, 0, 0))
     return pl.pallas_call(
         finish_kernel,
-        grid=(4,),
-        out_shape=tuple(jax.ShapeDtypeStruct((2,) + s, f32) for s in ((D, FF), (FF, D), (D, 3 * D), (D, D))),
-        in_specs=[pl.BlockSpec((D, D), index) for index in slabs for _ in range(2)],
-        out_specs=tuple(pl.BlockSpec((2, D, D), index) for index in targets),
+        grid=(WINDOW,),
+        out_shape=tuple(
+            jax.ShapeDtypeStruct(shape, f32)
+            for shape in [(2, D, FF), (2, FF, D), (2, D, 3 * D), (2, D, D)] + small_shapes
+        ) + tuple(jax.ShapeDtypeStruct(v.shape, v.dtype) for v in passed),
+        in_specs=[pl.BlockSpec((D, D), lambda j, row=row: (row(j), 0)) for row in first for _ in range(2)]
+        + [whole(small.shape)] + [tokens] * 2,
+        out_specs=tuple(pl.BlockSpec((2, D, D), place) for place in places) + tuple(whole(v) for v in small_shapes)
+        + (tokens,) * 2,
         compiler_params=params(),
         name="finish_gradients",
-    )(*[grads_one, grads_two] * 4)
+    )(*[grads_one, grads_two] * 4, small, *passed)
 
 
 def position_lookup():
@@ -833,27 +867,26 @@
     cells_of = lambda v: v.reshape(CELL + v.shape[1:])
     rows_of = lambda v: v.reshape((CELLS,) + v.shape[2:])
     x_first, x_last, cot_shifted, qw, pr, o16, mid, u = run_first(
-        crop_extent, x, cells_of(cot), norm_gain, norm_bias, qkv_weight, qv_bias, bias, proj_weight, out_bias,
+        crop_extent.T, x, cells_of(cot), norm_gain, norm_bias, qkv_weight, qv_bias, bias, proj_weight, out_bias,
         fc1_weight, fc1_bias, fc2_weight,
     )
     y, dx_first, dx_last, grads_two = run_second(
-        crop_extent, crop_counts, x_first, x_last, rows_of(cot_shifted), norm_gain, norm_bias, qkv_weight, qv_bias,
+        crop_extent.T, crop_counts, x_first, x_last, rows_of(cot_shifted), norm_gain, norm_bias, qkv_weight, qv_bias,
         bias, proj_weight, out_bias, fc1_weight, fc1_bias, fc2_weight,
     )
-    dx, sum_one, sum_two, output = run_third(
+    dx, sum_one, sum_two, output, small = run_third(
         x, dx_first, dx_last, cells_of(y), qw, pr, o16, mid, u, norm_gain, norm_bias, qkv_weight, proj_weight,
         fc1_weight, fc2_weight, grads_two,
     )
-    fc1, fc2, qkv, proj = finish(sum_one, sum_two)
-    rows = jnp.stack([sum_one[SLABS * D :], sum_two[SLABS * D :]]).astype(f32)
-    dbias = rows[:, SMALL : SMALL + TABLE, : 4 * SLOT].reshape(2, GROUPS, KEYS, 4, SLOT).transpose(0, 1, 3, 2, 4)
+    fc1, fc2, qkv, proj, gains, biases, qv, outs, fc1_b, output, dx = finish(
+        sum_one, sum_two, small, rows_of(output), dx
+    )
+    dbias = small[:, SMALL : SMALL + TABLE, : 4 * SLOT].astype(f32)
+    dbias = dbias.reshape(2, GROUPS, KEYS, 4, SLOT).transpose(0, 1, 3, 2, 4)
     table = jnp.einsum("hp,kp->kh", dbias.reshape(2 * HEADS, KEYS * SLOT), lookup, precision=highest)
     table = table.reshape(-1, 2, HEADS).transpose(1, 0, 2)
     back = lambda v: v.transpose(1, 0, 2).reshape(tokens.shape)
-    return (
-        back(rows_of(output)), back(dx), rows[:, 0:2], rows[:, 2:4], qkv, rows[:, 4:6], table, proj, rows[:, 6:8], fc1,
-        rows[:, 8:12].reshape(2, FF), fc2,
-    )
+    return back(output), back(dx), gains, biases, qkv, qv, table, proj, outs, fc1, fc1_b, fc2
 
 
 def solution(mesh):

time: 227 us -> 223 us (0.982)
  local copies, waits for them, and re-layouts: 10.5 us -> 4.22 us
  Pallas kernels: 211 us -> 214 us
    unnamed x12 -> x3, local copies, waits for them, and re-layouts: 5.35 us -> 0.65 us
    pallas_call x1, Pallas kernels: 8.73 us -> 11.7 us  [finish(): pl.pallas_call(finish_kernel, grid=(WINDOW,), out_shape=tuple((jax.ShapeD...]
where the time goes in v1:
time: 223 us; the launch traced here: 222 us
  Pallas kernels  214 us (96%)
  local copies, waits for them, and re-layouts  4.22 us (2%)
    pallas_call x1, Pallas kernels, run_third(): pl.pallas_call(third_kernel, grid=(4,), out_shape=(jax.ShapeDtypeStruct(x...  114 us
    pallas_call x1, Pallas kernels, run_second(): pl.pallas_call(second_kernel, grid=(2,), out_shape=(jax.ShapeDtypeStruct(...  61.5 us
    pallas_call x1, Pallas kernels, run_first(): pl.pallas_call(first_kernel, grid=(2,), out_shape=(PART, PART, jax.ShapeD...  27.1 us
    pallas_call x1, Pallas kernels, finish(): pl.pallas_call(finish_kernel, grid=(WINDOW,), out_shape=tuple((jax.ShapeD...  11.7 us

profile of v1, /device:TPU:0, one launch (start us, length us, event | category | flops | bytes accessed | tf_op | source)
XLA Modules:
  0.0 222.2 jit_solution(129159917254415488)
XLA Ops:
  0.6 0.0 copy-start
  1.4 0.1 add_select_fusion
  1.5 0.1 reshape.211
  1.5 0.0 copy-done
  1.5 1.1 fusion
  2.7 0.3 copy.31
  2.9 0.4 reshape.199
  3.4 0.1 select_bitcast_fusion
  3.5 0.3 copy.32
  3.8 1.2 reshape.200.bias
  4.9 27.1 %first_forward.1 = (bf16[7,7,16,384]{3,2,1,0:T(8,128)(2,1)}, bf16[7,7,16,384]{3,2,1,0:T(8,128)(2,1)}, bf16[7,7,32,384]{3,2,1,0:T(8,128)(2,1)}, bf16[32,9,64,128]...) custom-call(s32[2,32]{1,0:T(2,128)} %bitcast.46, ...), custom_call_target="tpu_custom_call" | custom-call | tf_op jit(solution)/shard_map/first_forward/pallas_call | solution.py:595
  32.0 61.5 %second_block.1 = (bf16[49,32,384]{2,1,0:T(8,128)(2,1)}, bf16[7,7,16,384]{3,2,1,0:T(8,128)(2,1)}, bf16[7,7,16,384]{3,2,1,0:T(8,128)(2,1)}, bf16[4864,384]{1,0:T(8,128)(2,1)}) custom-call(s32[2,32]{1,0:T(2,128)} %bitcast.47, s32[1]{0:T(128)S(6)} %copy.42.count, bf16[7,7,16,384]{3,2,1,0:T(8,128)(2,1)} %get-tuple-element.40.x_first, ...), custom_call_target="tpu_custom_call" | custom-call | tf_op jit(solution)/shard_map/second_block/pallas_call | solution.py:630
  93.6 114.0 %first_backward.1 = (bf16[49,32,384]{2,1,0:T(8,128)(2,1)}, bf16[4864,384]{1,0:T(8,128)(2,1)}, bf16[4864,384]{1,0:T(8,128)(2,1)}, bf16[7,7,32,384]{3,2,1,0:T(8,128)(2,1)}, bf16[2,256,384]{2,1,0:T(8,128)(2,1)}) custom-call(bf16[49,32,384]{2,1,0:T(8,128)(2,1)} %bitcast.40, bf16[7,7,16,384]{3,2,1,0:T(8,128)(2,1)} %get-tuple-element.43.dy_first, ...), custom_call_target="tpu_custom_call" | custom-call | tf_op jit(solution)/shard_map/first_backward/pallas_call | solution.py:659
  207.6 0.9 slice.3
  208.5 0.2 reshape.206
  208.8 0.2 dot_general.9
  209.0 0.6 fusion.7
  209.6 0.6 copy.35
  210.2 11.7 %finish_gradients.1 = (f32[2,384,1536]{2,1,0:T(8,128)}, f32[2,1536,384]{2,1,0:T(8,128)}, f32[2,384,1152]{2,1,0:T(8,128)}, f32[2,384,384]{2,1,0:T(8,128)}, f32[2,...) custom-call(bf16[4864,384]{1,0:T(8,128)(2,1)} %get-tuple-element.52., ...), custom_call_target="tpu_custom_call" | custom-call | tf_op jit(solution)/shard_map/finish_gradients/pallas_call | solution.py:829
  (5 shorter events, 0.1 us)
Async XLA Ops:
  0.6 0.9 copy-start

commit v2 on v1

--- a/solution.py
+++ b/solution.py
@@ -371,12 +371,13 @@
 
 def second_kernel(
     ext, count, x_first, x_last, cot_ref, gain, beta, wqkv, qvb, bias, wp, ob, w1, b1, w2,
-    y_ref, dx_shifted, dx_last, grads,
-    xs, qw, pr, os, mid, slope, dos, small, dbias, n1, n2, o16, z, dm, du, da, dp, x_both, dx_first, send, recv, local,
+    y_shifted, y_last, dx_shifted, dx_last, grads,
+    xs, qw, pr, os, mid, slope, dos, small, dbias, n1, n2, o16, z, dm, du, da, dp, x_both, dx_first, y_first, send, recv, local,
 ):
     step = pl.program_id(0)
     x_copies = shift_copies(x_last, x_both.at[1], send.at[0], recv.at[0])
     dx_copies = shift_copies(dx_first, dx_shifted, send.at[1], recv.at[1], back=True)
+    y_copies = shift_copies(y_first, y_shifted, send.at[2], recv.at[2], back=True)
 
     @pl.when(step == 0)
     def _():
@@ -401,7 +402,17 @@
         (ext, gain, beta, wqkv, qvb, bias, wp, ob, w1, b1, w2, xs, qw, pr, os, o16.at[step], mid),
         n1, n2, (z, slope),
     )
-    y_ref[...] = jnp.where(live, y.reshape(CELLS, HALF, D), 0.0).astype(bf16)
+    y = jnp.where(live, y.reshape(CELLS, HALF, D), 0.0).astype(bf16).reshape(WINDOW, WINDOW, HALF, D)
+
+    @pl.when(step == 0)
+    def _():
+        y_first[...] = y
+        start_all(y_copies)
+
+    @pl.when(step == 1)
+    def _():
+        y_last[...] = y
+
     dy = jnp.where(live, cot_ref[...].astype(f32), 0.0).reshape(ROWS, D)
     mid[...] = mlp_back(
         step, 1, mid[...], dy, (gain, wp, w1, w2, dos, dm, du, da, small), lambda cut: slope[:, cut].astype(f32)
@@ -422,6 +433,7 @@
         fc_grads(n2, z, dm, du, grads)
         attention_grads(n1, o16, da, dp, grads)
         small_grads(small, dbias, grads)
+        wait_all(y_copies)
         wait_all(dx_copies)
 
 
@@ -587,7 +599,7 @@
 
 CELL = (WINDOW, WINDOW)
 PART = jax.ShapeDtypeStruct(CELL + (HALF, D), bf16)
-SHIFTS = [pltpu.SemaphoreType.DMA((2, 4)), pltpu.SemaphoreType.DMA((2, 4))]
+SHIFTS = [pltpu.SemaphoreType.DMA((3, 4)), pltpu.SemaphoreType.DMA((3, 4))]
 
 
 def run_first(ext, x, cot, gain, beta, wqkv, qvb, bias, wp, ob, w1, b1, w2):
@@ -630,18 +642,19 @@
     return pl.pallas_call(
         second_kernel,
         grid=(2,),
-        out_shape=(jax.ShapeDtypeStruct(cot.shape, bf16), PART, PART, GRADS),
+        out_shape=(PART, PART, PART, PART, GRADS),
         in_specs=[
             SMEM_SPEC, SMEM_SPEC, ANY_SPEC, ANY_SPEC, TOKEN_SPEC, whole(gain.shape), whole(beta.shape), of_block(1, D, 3 * D),
             whole(qvb.shape), of_block(1, GROUPS, KEYS, 4 * SLOT), of_block(1, D, D), whole(ob.shape),
             of_block(1, D, FF), whole(b1.shape), of_block(1, FF, D),
         ],
-        out_specs=(TOKEN_SPEC, ANY_SPEC, whole(PART.shape), whole(GRADS.shape)),
+        out_specs=(ANY_SPEC, whole(PART.shape), ANY_SPEC, whole(PART.shape), whole(GRADS.shape)),
         scratch_shapes=[
             XS, VMEM(QW, bf16), VMEM(PR, bf16), VMEM((2, GROUPS, 8 * KEYS, LANES), f32),
             VMEM((ROWS, D), f32), VMEM((ROWS, FF), bf16), DOS,
         ] + SMALLS + [VMEM((2, ROWS, width), bf16) for width in (D, D, D, FF, D, FF, D, 3 * D)]
-        + [VMEM((2,) + PART.shape, bf16), VMEM(PART.shape, bf16)] + SHIFTS + [pltpu.SemaphoreType.DMA(())],
+        + [VMEM((2,) + PART.shape, bf16), VMEM(PART.shape, bf16), VMEM(PART.shape, bf16)] + SHIFTS
+        + [pltpu.SemaphoreType.DMA(())],
         compiler_params=params(2, 63),
         name="second_block",
     )(ext, count, x_first, x_last, cot, gain, beta, wqkv, qvb, bias, wp, ob, w1, b1, w2)
@@ -796,7 +809,8 @@
 
 
 def finish_kernel(*refs):
-    ins, (small, *sources), outs, smalls, targets = refs[:8], refs[8:11], refs[11:15], refs[15:20], refs[20:22]
+    ins, (small, *parts, dx), outs, smalls = refs[:8], refs[8:12], refs[12:16], refs[16:21]
+    y_out, dx_out = refs[21:]
     step = pl.program_id(0)
 
     @pl.when(step == 0)
@@ -807,8 +821,9 @@
         for n in range(4):
             smalls[4][:, D * n : D * (n + 1)] = rows[:, 8 + n]
 
-    for source, target in zip(sources, targets):
-        target[...] = source[...]
+    for n, part in enumerate(parts):
+        y_out[:, HALF * n : HALF * (n + 1)] = part[...]
+    dx_out[...] = dx[...]
 
     @pl.when(step < 4)
     def _():
@@ -818,28 +833,28 @@
                 out[block] = value.T if n == 1 else value
 
 
-def finish(grads_one, grads_two, small, *passed):
+def finish(grads_one, grads_two, small, y_first, y_last, dx):
     first = [lambda j: jnp.minimum(j, 3), lambda j: 4 + jnp.minimum(j, 3), lambda j: 8 + jnp.minimum(j, 2), lambda j: 11]
     places = [
         lambda j: (0, 0, jnp.minimum(j, 3)), lambda j: (0, jnp.minimum(j, 3), 0), lambda j: (0, 0, jnp.minimum(j, 2)),
         lambda j: (0, 0, 0),
     ]
     small_shapes = [(2, 2, D)] * 4 + [(2, FF)]
-    tokens = pl.BlockSpec((WINDOW,) + passed[0].shape[1:], lambda j: (j, 0, 0))
+    tokens, part = (pl.BlockSpec((WINDOW,) + v.shape[1:], lambda j: (j, 0, 0)) for v in (dx, y_first))
     return pl.pallas_call(
         finish_kernel,
         grid=(WINDOW,),
         out_shape=tuple(
             jax.ShapeDtypeStruct(shape, f32)
             for shape in [(2, D, FF), (2, FF, D), (2, D, 3 * D), (2, D, D)] + small_shapes
-        ) + tuple(jax.ShapeDtypeStruct(v.shape, v.dtype) for v in passed),
+        ) + (jax.ShapeDtypeStruct(dx.shape, bf16),) * 2,
         in_specs=[pl.BlockSpec((D, D), lambda j, row=row: (row(j), 0)) for row in first for _ in range(2)]
-        + [whole(small.shape)] + [tokens] * 2,
+        + [whole(small.shape), part, part, tokens],
         out_specs=tuple(pl.BlockSpec((2, D, D), place) for place in places) + tuple(whole(v) for v in small_shapes)
         + (tokens,) * 2,
         compiler_params=params(),
         name="finish_gradients",
-    )(*[grads_one, grads_two] * 4, small, *passed)
+    )(*[grads_one, grads_two] * 4, small, y_first, y_last, dx)
 
 
 def position_lookup():
@@ -870,16 +885,16 @@
         crop_extent.T, x, cells_of(cot), norm_gain, norm_bias, qkv_weight, qv_bias, bias, proj_weight, out_bias,
         fc1_weight, fc1_bias, fc2_weight,
     )
-    y, dx_first, dx_last, grads_two = run_second(
+    y_first, y_last, dx_first, dx_last, grads_two = run_second(
         crop_extent.T, crop_counts, x_first, x_last, rows_of(cot_shifted), norm_gain, norm_bias, qkv_weight, qv_bias,
         bias, proj_weight, out_bias, fc1_weight, fc1_bias, fc2_weight,
     )
-    dx, sum_one, sum_two, output, small = run_third(
-        x, dx_first, dx_last, cells_of(y), qw, pr, o16, mid, u, norm_gain, norm_bias, qkv_weight, proj_weight,
+    dx, sum_one, sum_two, y_last, small = run_third(
+        x, dx_first, dx_last, y_last, qw, pr, o16, mid, u, norm_gain, norm_bias, qkv_weight, proj_weight,
         fc1_weight, fc2_weight, grads_two,
     )
     fc1, fc2, qkv, proj, gains, biases, qv, outs, fc1_b, output, dx = finish(
-        sum_one, sum_two, small, rows_of(output), dx
+        sum_one, sum_two, small, rows_of(y_first), rows_of(y_last), dx
     )
     dbias = small[:, SMALL : SMALL + TABLE, : 4 * SLOT].astype(f32)
     dbias = dbias.reshape(2, GROUPS, KEYS, 4, SLOT).transpose(0, 1, 3, 2, 4)

time: 223 us -> 219 us (0.982)
  Pallas kernels: 214 us -> 210 us
    pallas_call x1, Pallas kernels: 114 us -> 109 us  [run_third(): pl.pallas_call(third_kernel, grid=(4,), out_shape=(jax.ShapeDtypeStruct(x...]
where the time goes in v2:
time: 219 us; the launch traced here: 218 us
  Pallas kernels  210 us (96%)
  local copies, waits for them, and re-layouts  4.22 us (2%)
    pallas_call x1, Pallas kernels, run_third(): pl.pallas_call(third_kernel, grid=(4,), out_shape=(jax.ShapeDtypeStruct(x...  109 us
    pallas_call x1, Pallas kernels, run_second(): pl.pallas_call(second_kernel, grid=(2,), out_shape=(PART, PART, PART, PAR...  62.1 us
    pallas_call x1, Pallas kernels, run_first(): pl.pallas_call(first_kernel, grid=(2,), out_shape=(PART, PART, jax.ShapeD...  27.1 us
    pallas_call x1, Pallas kernels, finish(): pl.pallas_call(finish_kernel, grid=(WINDOW,), out_shape=tuple((jax.ShapeD...  11.7 us

profile of v2, /device:TPU:0, one launch (start us, length us, event | category | flops | bytes accessed | tf_op | source)
XLA Modules:
  0.0 217.6 jit_solution(4789647903684871599)
XLA Ops:
  0.6 0.0 copy-start
  1.4 0.1 add_select_fusion
  1.5 0.1 reshape.211
  1.5 0.0 copy-done
  1.5 1.1 fusion
  2.7 0.3 copy.31
  2.9 0.4 reshape.199
  3.4 0.1 select_bitcast_fusion
  3.5 0.3 copy.32
  3.8 1.2 reshape.200.bias
  4.9 27.1 %first_forward.1 = (bf16[7,7,16,384]{3,2,1,0:T(8,128)(2,1)}, bf16[7,7,16,384]{3,2,1,0:T(8,128)(2,1)}, bf16[7,7,32,384]{3,2,1,0:T(8,128)(2,1)}, bf16[32,9,64,128]...) custom-call(s32[2,32]{1,0:T(2,128)} %bitcast.46, ...), custom_call_target="tpu_custom_call" | custom-call | tf_op jit(solution)/shard_map/first_forward/pallas_call | solution.py:607
  32.0 62.1 %second_block.1 = (bf16[7,7,16,384]{3,2,1,0:T(8,128)(2,1)}, bf16[7,7,16,384]{3,2,1,0:T(8,128)(2,1)}, bf16[7,7,16,384]{3,2,1,0:T(8,128)(2,1)}, bf16[7,7,16,384]{3,2,1,0:T(8,128)(2,1)}, bf16[4864,384]{1,0:T(8,128)(2,1)}) custom-call(s32[2,32]{1,0:T(2,128)} %bitcast.47, s32[1]{0:T(128)S(6)} %copy.42.count, bf16[7,7,16,384]{3,2,1,0:T(8,128)(2,1)} %get-tuple-element.41.x_first, ...), custom_call_target="tpu_custom_call" | custom-call | tf_op jit(solution)/shard_map/second_block/pallas_call | solution.py:642
  94.1 108.9 %first_backward.1 = (bf16[49,32,384]{2,1,0:T(8,128)(2,1)}, bf16[4864,384]{1,0:T(8,128)(2,1)}, bf16[4864,384]{1,0:T(8,128)(2,1)}, bf16[7,7,16,384]{3,2,1,0:T(8,128)(2,1)}, bf16[2,256,384]{2,1,0:T(8,128)(2,1)}) custom-call(bf16[49,32,384]{2,1,0:T(8,128)(2,1)} %bitcast.40, bf16[7,7,16,384]{3,2,1,0:T(8,128)(2,1)} %get-tuple-element.44.dy_first, ...), custom_call_target="tpu_custom_call" | custom-call | tf_op jit(solution)/shard_map/first_backward/pallas_call | solution.py:672
  203.0 0.9 slice.3
  203.9 0.2 reshape.206
  204.2 0.2 dot_general.9
  204.4 0.6 fusion.7
  205.0 0.6 copy.35
  205.6 11.7 %finish_gradients.1 = (f32[2,384,1536]{2,1,0:T(8,128)}, f32[2,1536,384]{2,1,0:T(8,128)}, f32[2,384,1152]{2,1,0:T(8,128)}, f32[2,384,384]{2,1,0:T(8,128)}, f32[2,...) custom-call(bf16[4864,384]{1,0:T(8,128)(2,1)} %get-tuple-element.53., ...), custom_call_target="tpu_custom_call" | custom-call | tf_op jit(solution)/shard_map/finish_gradients/pallas_call | solution.py:844
  (5 shorter events, 0.1 us)
Async XLA Ops:
  0.6 0.9 copy-start

commit v3 on v2

--- a/solution.py
+++ b/solution.py
@@ -23,7 +23,7 @@
 SMALL = 16
 TABLE = GROUPS * KEYS
 SUMS = SLABS * D + 256
-GROUPED = ((0, 1), (2, 3), (4, 5, 6))
+GROUPED = ((1, 0), (3, 2), (5, 4, 6))
 NEG = -1e30
 LOG2E = 1.4426950408889634
 SCALE = HEAD_DIM**-0.5

time: 219 us -> 219 us (level)
  no operation moved by 1% of the time
where the time goes in v3:
time: 219 us; the launch traced here: 218 us
  Pallas kernels  210 us (96%)
  local copies, waits for them, and re-layouts  4.22 us (2%)
    pallas_call x1, Pallas kernels, run_third(): pl.pallas_call(third_kernel, grid=(4,), out_shape=(jax.ShapeDtypeStruct(x...  110 us
    pallas_call x1, Pallas kernels, run_second(): pl.pallas_call(second_kernel, grid=(2,), out_shape=(PART, PART, PART, PAR...  62.1 us
    pallas_call x1, Pallas kernels, run_first(): pl.pallas_call(first_kernel, grid=(2,), out_shape=(PART, PART, jax.ShapeD...  27.1 us
    pallas_call x1, Pallas kernels, finish(): pl.pallas_call(finish_kernel, grid=(WINDOW,), out_shape=tuple((jax.ShapeD...  11.7 us

profile of v3, /device:TPU:0, one launch (start us, length us, event | category | flops | bytes accessed | tf_op | source)
XLA Modules:
  0.0 218.3 jit_solution(2751999894508911703)
XLA Ops:
  0.6 0.0 copy-start
  1.4 0.1 add_select_fusion
  1.5 0.1 reshape.211
  1.5 0.0 copy-done
  1.5 1.1 fusion
  2.7 0.3 copy.31
  2.9 0.4 reshape.199
  3.4 0.1 select_bitcast_fusion
  3.5 0.3 copy.32
  3.8 1.2 reshape.200.bias
  4.9 27.1 %first_forward.1 = (bf16[7,7,16,384]{3,2,1,0:T(8,128)(2,1)}, bf16[7,7,16,384]{3,2,1,0:T(8,128)(2,1)}, bf16[7,7,32,384]{3,2,1,0:T(8,128)(2,1)}, bf16[32,9,64,128]...) custom-call(s32[2,32]{1,0:T(2,128)} %bitcast.46, ...), custom_call_target="tpu_custom_call" | custom-call | tf_op jit(solution)/shard_map/first_forward/pallas_call | solution.py:607
  32.0 62.1 %second_block.1 = (bf16[7,7,16,384]{3,2,1,0:T(8,128)(2,1)}, bf16[7,7,16,384]{3,2,1,0:T(8,128)(2,1)}, bf16[7,7,16,384]{3,2,1,0:T(8,128)(2,1)}, bf16[7,7,16,384]{3,2,1,0:T(8,128)(2,1)}, bf16[4864,384]{1,0:T(8,128)(2,1)}) custom-call(s32[2,32]{1,0:T(2,128)} %bitcast.47, s32[1]{0:T(128)S(6)} %copy.42.count, bf16[7,7,16,384]{3,2,1,0:T(8,128)(2,1)} %get-tuple-element.41.x_first, ...), custom_call_target="tpu_custom_call" | custom-call | tf_op jit(solution)/shard_map/second_block/pallas_call | solution.py:642
  94.1 109.6 %first_backward.1 = (bf16[49,32,384]{2,1,0:T(8,128)(2,1)}, bf16[4864,384]{1,0:T(8,128)(2,1)}, bf16[4864,384]{1,0:T(8,128)(2,1)}, bf16[7,7,16,384]{3,2,1,0:T(8,128)(2,1)}, bf16[2,256,384]{2,1,0:T(8,128)(2,1)}) custom-call(bf16[49,32,384]{2,1,0:T(8,128)(2,1)} %bitcast.40, bf16[7,7,16,384]{3,2,1,0:T(8,128)(2,1)} %get-tuple-element.44.dy_first, ...), custom_call_target="tpu_custom_call" | custom-call | tf_op jit(solution)/shard_map/first_backward/pallas_call | solution.py:672
  203.7 0.9 slice.3
  204.6 0.2 reshape.206
  204.9 0.2 dot_general.9
  205.1 0.6 fusion.7
  205.7 0.6 copy.35
  206.3 11.7 %finish_gradients.1 = (f32[2,384,1536]{2,1,0:T(8,128)}, f32[2,1536,384]{2,1,0:T(8,128)}, f32[2,384,1152]{2,1,0:T(8,128)}, f32[2,384,384]{2,1,0:T(8,128)}, f32[2,...) custom-call(bf16[4864,384]{1,0:T(8,128)(2,1)} %get-tuple-element.53., ...), custom_call_target="tpu_custom_call" | custom-call | tf_op jit(solution)/shard_map/finish_gradients/pallas_call | solution.py:844
  (5 shorter events, 0.1 us)
Async XLA Ops:
  0.6 0.9 copy-start
